TPU v7x, 32 devices: a whole 2x2x4 slice. The times are simulated.
32 devices in a mesh: chan: 8 (over z, x), kred: 4 (over y, core).
Axes of the slice: x: 2, y: 2, z: 4, core: 2. Of those that a mesh axis runs over, the one named last changes fastest.
Arguments:
- t2_ph: bfloat16 [8, 4096, 128], P('chan', 'kred'), may hold values from -6 to 6
- dest_owner: int32 [8, 4096], P('chan', 'kred'), may hold values from 0 to 7, as said below
- source_owner: int32 [8, 4096], P('chan', 'kred'), may hold values from 0 to 7, as said below
- source_slot: int32 [8, 4096], P('chan', 'kred'), may hold values from 0 to 255
- hole_count: int32 [8], P('chan'), may hold values from 32 to 128
- ladder_v: bfloat16 [8, 4096, 4096], P('chan', None, 'kred'), as said below
Outputs:
- ladder_out: bfloat16 [8, 4096, 128], P('chan', 'kred')
Inputs may be any that keep to these rules, and one draw needn't show every extreme that they name: Within each aligned block of 1024 rows of dest_owner[s] at most 256 rows name the same channel, and some channel is named by exactly 256; every channel is named by exactly 1024 rows of the same block index over all s. The pairs (source_owner, source_slot) of one channel and one aligned block of 1024 columns are distinct and name exactly the rows that dest_owner sends to that channel from that block. `ladder_v`: symmetric in its last two dimensions for each channel.
All inputs are finite; a program needn't handle non-finite values.
Results may differ from a plain program's by a relative error of at most 0.001.
Values may be sent and summed in bfloat16 or wider, within the bound.
A program may use at most 64 MiB of HBM per device.

v0:
```python
import jax
import jax.numpy as jnp
from jax import lax
from jax.sharding import PartitionSpec as P


def on_device(t2_ph, dest_owner, source_owner, source_slot, hole_count, ladder_v):
    ph_rows = t2_ph[0]
    owners = dest_owner[0]
    owners_count = lax.axis_size("chan")
    slab_rows = ph_rows.shape[0]
    hole_width = ph_rows.shape[1]
    capacity = 2 * slab_rows // owners_count
    matches = (owners[:, None] == jnp.arange(owners_count, dtype=jnp.int32)[None, :]).astype(
        jnp.int32
    )
    before = jnp.sum((jnp.cumsum(matches, axis=0) - matches) * matches, axis=1)
    target = owners * capacity + before
    outbox = jnp.zeros((owners_count * capacity, hole_width), ph_rows.dtype).at[target].set(ph_rows)
    arrived = lax.all_to_all(
        outbox.reshape(owners_count, capacity, hole_width),
        "chan",
        split_axis=0,
        concat_axis=0,
        tiled=True,
    )
    picked = source_owner[0] * capacity + source_slot[0]
    recoupled = arrived.reshape(owners_count * capacity, hole_width)[picked]
    weights = ladder_v[0]
    ladder = lax.dot_general(
        weights,
        lax.all_gather(recoupled, "kred", axis=0, tiled=True),
        (((0,), (0,)), ((), ())),
        preferred_element_type=jnp.float32,
    )
    columns = jnp.arange(hole_width, dtype=jnp.int32)
    masked = jnp.where(columns[None, :] < hole_count[0], ladder, jnp.float32(0.0))
    return masked.astype(jnp.bfloat16)[None]


def solution(mesh):
    placed = (
        P("chan", "kred", None),
        P("chan", "kred"),
        P("chan", "kred"),
        P("chan", "kred"),
        P("chan"),
        P("chan", None, "kred"),
    )
    return jax.shard_map(
        on_device, mesh=mesh, in_specs=placed, out_specs=P("chan", "kred", None), check_vma=False
    )
```

profile of v0, /device:TPU:0, one launch (start us, length us, event | category | flops | bytes accessed | tf_op | source)
XLA Modules:
  0.0 70.2 jit_solution(12383545056537703978)
XLA Ops:
  6.5 0.0 copy-start
  6.5 0.7 %fusion.17 = s32[8,8,128]{2,1,0:T(8,128)S(1)} fusion(s32[8,128]{1,0:T(8,128)} %bitcast.52), kind=kLoop, calls=%fused_computation.18 | loop fusion | flops 16384 | bytes 36864 | tf_op jit(solution)/shard_map/convert_element_type | solution.py:14
  7.3 2.3 %reduce-window.6 = s32[8,8,128]{2,1,0:T(8,128)S(1)} reduce-window(s32[8,8,128]{2,1,0:T(8,128)S(1)} %fusion.17, s32[]{:T(128)} %constant.3.clone.1), window={size=1x1x128 pad=0_0x0_0x127_0}, to_apply=%region_0.0 | reduce-window | flops 1040384 | bytes 65540 | tf_op jit(solution)/shard_map/reduce-window
  9.5 0.3 slice_reduce_fusion
  9.8 0.2 reduce-window.9
  10.0 0.1 add_bitcast_fusion
  10.0 0.7 %fusion.16 = s32[1024]{0:T(1024)S(1)} fusion(s32[1,8,8,128]{3,2,1,0:T(8,128)S(1)} %add_bitcast_fusion, s32[1024]{0:T(1024)} %bitcast.53), kind=kLoop, calls=%fused_computation.13 | loop fusion | flops 39936 | bytes 40960 | tf_op jit(solution)/shard_map/reduce_sum | solution.py:17
  10.8 0.7 compare_select_fusion.1
  11.5 0.0 copy-done
  11.5 4.0 %scatter_custom_fusion = bf16[2048,128]{1,0:T(8,128)(2,1)} fusion(s32[1024]{0:T(1024)S(1)} %bitcast.57, bf16[1,1024,128]{2,1,0:T(8,128)(2,1)S(1)} %copy-done, bf16[]{:T(256)} %constant.5.clone.1), kind=kCustom, calls=%fused_computation.7 | custom fusion | bytes 786434 | tf_op jit(solution)/shard_map/scatter | solution.py:19
  15.5 7.3 %all-to-all-start = ((bf16[8,256,128]{2,1,0:T(8,128)(2,1)}), bf16[8,256,128]{2,1,0:T(8,128)(2,1)S(1)}, u32[]{:S(2)}, u32[]{:S(2)}) async-start(bf16[8,256,128]{2,1,0:T(8,128)(2,1)} %bitcast.8), calls=%async_computation | async-start | bytes 1048576 | tf_op jit(solution)/shard_map/all_to_all | solution.py:20
  22.7 0.0 all-gather.3.cloned.1.call-start
  22.8 0.7 %compare_select_fusion = s32[1024,1]{0,1:T(1,128)S(1)} fusion(s32[1,1024]{1,0:T(1,128)} %param.9, s32[1,1024]{1,0:T(1,128)} %param.8), kind=kLoop, calls=%fused_computation.19 | loop fusion | flops 5120 | bytes 12288 | tf_op jit(solution)/shard_map/select_n | solution.py:28
  23.5 13.7 %all-to-all-done = bf16[8,256,128]{2,1,0:T(8,128)(2,1)S(1)} async-done(((bf16[8,256,128]{2,1,0:T(8,128)(2,1)}), bf16[8,256,128]{2,1,0:T(8,128)(2,1)S(1)}, u32[]{:S(2)}, u32[]{:S(2)}) %all-to-all-start) | async-done | bytes 524320 | tf_op jit(solution)/shard_map/all_to_all | solution.py:20
  37.2 4.3 %gather_fusion = bf16[1024,128]{1,0:T(8,128)(2,1)} fusion(bf16[2048,128]{1,0:T(8,128)(2,1)S(1)} %bitcast.51, s32[1024]{0:T(1024)S(1)} %broadcast_clamp_fusion), kind=kCustom, calls=%fused_computation | custom fusion | bytes 528384 | tf_op jit(solution)/shard_map/gather | solution.py:28
  41.5 0.0 all-gather.3.cloned.1.call-update
  42.2 15.3 %all-gather.3.cloned.1.call-done = bf16[4096,128]{1,0:T(8,128)(2,1)} async-done(((bf16[1024,128]{1,0:T(8,128)(2,1)}), bf16[4096,128]{1,0:T(8,128)(2,1)}) %all-gather.3.cloned.1.call-update) | async-done | bytes 1048592 | tf_op jit(solution)/shard_map/all_gather | solution.py:32
  57.5 5.0 %fusion.8 = bf16[1,1024,128]{1,2,0:T(8,128)(2,1)S(1)} fusion(bf16[4096,128]{1,0:T(8,128)(2,1)} %all-gather.3.cloned.1.call-done, bf16[1,4096,1024]{2,1,0:T(8,128)(2,1)} %param.11, pred[128]{0:T(512)(128)(4,1)S(1)} %iota_compare_fusion.2), kind=kOutput, calls=%fused_computation.6 | convolution fusion | flops 1074003968 | bytes 9699456 | tf_op jit(solution)/shard_map/dot_general | solution.py:30
  62.5 0.8 %copy.8 = bf16[1,1024,128]{2,1,0:T(8,128)(2,1)} copy(bf16[1,1024,128]{1,2,0:T(8,128)(2,1)S(1)} %fusion.8) | data formatting | bytes 524288 | tf_op jit(solution)/shard_map/broadcast_in_dim | solution.py:38
  (2 shorter events, 0.0 us)
Async XLA Ops:
  6.5 4.9 %copy-start = (bf16[1,1024,128]{2,1,0:T(8,128)(2,1)S(1)}, bf16[1,1024,128]{2,1,0:T(8,128)(2,1)}, u32[]{:S(2)}) copy-start(bf16[1,1024,128]{2,1,0:T(8,128)(2,1)} %param.6) | copy-start | bytes 786436
  15.5 21.7 %all-to-all-start = ((bf16[8,256,128]{2,1,0:T(8,128)(2,1)}), bf16[8,256,128]{2,1,0:T(8,128)(2,1)S(1)}, u32[]{:S(2)}, u32[]{:S(2)}) async-start(bf16[8,256,128]{2,1,0:T(8,128)(2,1)} %bitcast.8), calls=%async_computation | async-start | bytes 1048576 | tf_op jit(solution)/shard_map/all_to_all | solution.py:20
  22.7 34.8 %all-gather.3.cloned.1.call-start = ((), (), s32[]{:S(2)}) async-start(), calls=%async_computation.1 | async-start | bytes 1310720 | tf_op jit(solution)/shard_map/all_gather | solution.py:32
Sparse Core Ops, SparseCore 0:
  41.6 15.7 all-gather.2
where the time goes:
time: 70.5 us; the launch traced here: 70.2 us
  waiting for transfers between devices  29 us (41%)
  between operations  14.1 us (20%)
  local copies, waits for them, and re-layouts  9.41 us (13%)
  starting transfers between devices  7.29 us (10%)
  other arithmetic  5.36 us (8%)
  matrix products  4.99 us (7%)
    all_gather x1, waiting for transfers between devices, on_device(): lax.all_gather(recoupled, 'kred', axis=0, tiled=True)  15.3 us
    all_to_all x1, waiting for transfers between devices, on_device(): lax.all_to_all(outbox.reshape(owners_count, capacity, hole_width), 'chan'...  13.7 us
    all_to_all x1, starting transfers between devices, on_device(): lax.all_to_all(outbox.reshape(owners_count, capacity, hole_width), 'chan'...  7.25 us
    dot_general x1, matrix products, on_device(): lax.dot_general(weights, lax.all_gather(recoupled, 'kred', axis=0, tiled=...  4.99 us
    gather x1, local copies, waits for them, and re-layouts, on_device(): recoupled = arrived.reshape(owners_count * capacity, hole_width)[picked]  4.31 us
    scatter x1, local copies, waits for them, and re-layouts, on_device(): jnp.zeros((owners_count * capacity, hole_width), ph_rows.dtype).at[target]  3.98 us
    another operation x2, other arithmetic  2.41 us
  transfers between devices with their start and end apart: 2, of which 2 were waited for; matrix products, arithmetic and copies ran while one was open for 1% of the time, Pallas kernels for 0%

commit v1 on v0

v1 whole, which is shorter than its diff:
```python
import functools

import jax
import jax.numpy as jnp
from jax import lax
from jax.experimental import pallas as pl
from jax.experimental.pallas import tpu as pltpu
from jax.sharding import PartitionSpec as P

MESH = pl.DeviceIdType.MESH
F32 = jnp.float32
BF16 = jnp.bfloat16


def one_hot(count, row):
    lanes = row.shape[1]
    index = lax.broadcasted_iota(jnp.int32, (count, lanes), 0)
    if count <= 256:
        hit = index.astype(F32).astype(BF16) == row.astype(F32).astype(BF16)
    else:
        hit = index == row
    return jnp.where(hit, jnp.ones((), BF16), jnp.zeros((), BF16))


def row_numbers(owners, n_chan):
    rows = owners.shape[1]
    blocks = rows // 128
    channel = lax.broadcasted_iota(jnp.int32, (n_chan, 128), 0)
    hits = [
        (owners[:, b * 128 : (b + 1) * 128] == channel).astype(F32) for b in range(blocks)
    ]
    above = lax.broadcasted_iota(jnp.int32, (128, 128), 0) < lax.broadcasted_iota(
        jnp.int32, (128, 128), 1
    )
    inside = jnp.dot(
        jnp.concatenate(hits, axis=0).astype(BF16),
        jnp.where(above, 1.0, 0.0).astype(BF16),
        preferred_element_type=F32,
    )
    numbers = []
    offset = jnp.zeros((n_chan, 1), F32)
    for b in range(blocks):
        here = inside[b * n_chan : (b + 1) * n_chan] + offset
        numbers.append(jnp.sum(here * hits[b], axis=0, keepdims=True))
        offset = offset + jnp.sum(hits[b], axis=1, keepdims=True)
    return jnp.concatenate(numbers, axis=1).astype(jnp.int32)


def kernel(
    n_chan,
    n_kred,
    t2_ref,
    dest_ref,
    owner_ref,
    slot_ref,
    hole_ref,
    v_hbm,
    out_ref,
    outbox,
    arrived,
    picks,
    slabs,
    v_ref,
    acc,
    part,
    v_sem,
    a_send,
    a_recv,
    y_send,
    y_recv,
    s_send,
    s_recv,
    f_send,
    f_recv,
):
    chan = lax.axis_index("chan")
    kred = lax.axis_index("kred")
    n_outer = n_kred // 2
    inner = kred % 2
    outer = kred // 2
    sibling = {"kred": outer * 2 + (1 - inner)}
    capacity = outbox.shape[1]
    slab = t2_ref.shape[1]
    pieces, wide = slabs.shape[1], slabs.shape[3]

    barrier = pltpu.get_barrier_semaphore()
    for o in range(1, n_chan):
        pl.semaphore_signal(
            barrier, inc=1, device_id={"chan": (chan + o) % n_chan}, device_id_type=MESH
        )
    pl.semaphore_signal(barrier, inc=1, device_id=sibling, device_id_type=MESH)
    for d in range(1, n_outer):
        pl.semaphore_signal(
            barrier,
            inc=1,
            device_id={"kred": ((outer + d) % n_outer) * 2 + inner},
            device_id_type=MESH,
        )

    load_v = pltpu.make_async_copy(v_hbm.at[0], v_ref, v_sem)
    load_v.start()

    owners = dest_ref[...]
    numbers = row_numbers(owners, n_chan)
    order = sorted(range(1, n_chan), key=lambda o: abs(2 * o - n_chan))
    rows = t2_ref[0]

    def packed(channel):
        choose = one_hot(capacity, jnp.where(owners == channel, numbers, -1))
        return jnp.dot(choose, rows, preferred_element_type=F32).astype(BF16)

    sends = {}
    for at, o in enumerate(order):
        partner = (chan + o) % n_chan
        outbox[o] = packed(partner)
        if at == 0:
            pl.semaphore_wait(barrier, n_chan - 1 + 1 + n_outer - 1)
        sends[o] = pltpu.make_async_remote_copy(
            src_ref=outbox.at[o],
            dst_ref=arrived.at[o],
            send_sem=a_send.at[o],
            recv_sem=a_recv.at[o],
            device_id={"chan": partner},
            device_id_type=MESH,
        )
        sends[o].start()
    own = packed(chan)

    source = owner_ref[...]
    slots = slot_ref[...]
    for o in range(n_chan):
        sender = (chan - o + n_chan) % n_chan
        picks[o] = one_hot(capacity, jnp.where(source == sender, slots, -1))

    def spread(block, o, cols):
        return lax.dot_general(
            block, picks[o, :, cols], (((0,), (0,)), ((), ())), preferred_element_type=F32
        )

    last = order[-1]
    part[...] = spread(own, 0, slice(0, slab))
    for o in order[:-1]:
        sends[o].wait_recv()
        part[...] += spread(arrived[o], o, slice(0, slab))
    if order:
        sends[last].wait_recv()
    across, beside = {}, {}
    for i in range(pieces):
        cols = slice(i * wide, (i + 1) * wide)
        piece = part[:, cols] + spread(arrived[last], last, cols)
        slabs[0, i] = piece.astype(BF16)
        for d in range(1, n_outer):
            across[d, i] = pltpu.make_async_remote_copy(
                src_ref=slabs.at[0, i],
                dst_ref=slabs.at[2 * d, i],
                send_sem=y_send.at[d, i],
                recv_sem=y_recv.at[d, i],
                device_id={"kred": ((outer + d) % n_outer) * 2 + inner},
                device_id_type=MESH,
            )
            across[d, i].start()
        beside[i] = pltpu.make_async_remote_copy(
            src_ref=slabs.at[0, i],
            dst_ref=slabs.at[1, i],
            send_sem=s_send.at[i],
            recv_sem=s_recv.at[i],
            device_id=sibling,
            device_id_type=MESH,
        )
        beside[i].start()

    def product(place, i, index):
        start = pl.multiple_of(index * slab + i * wide, wide)
        return jnp.dot(
            slabs[place, i], v_ref[pl.ds(start, wide), :], preferred_element_type=F32
        )

    load_v.wait()
    acc[...] = product(0, 0, kred)
    for i in range(1, pieces):
        acc[...] += product(0, i, kred)
    for i in range(pieces):
        beside[i].wait_recv()
        acc[...] += product(1, i, outer * 2 + (1 - inner))
    onward = {}
    for d in range(1, n_outer):
        from_outer = (outer - d + n_outer) % n_outer
        for i in range(pieces):
            across[d, i].wait_recv()
            onward[d, i] = pltpu.make_async_remote_copy(
                src_ref=slabs.at[2 * d, i],
                dst_ref=slabs.at[2 * d + 1, i],
                send_sem=f_send.at[d, i],
                recv_sem=f_recv.at[d, i],
                device_id=sibling,
                device_id_type=MESH,
            )
            onward[d, i].start()
            acc[...] += product(2 * d, i, from_outer * 2 + inner)
            onward[d, i].wait_recv()
            acc[...] += product(2 * d + 1, i, from_outer * 2 + (1 - inner))

    live = lax.broadcasted_iota(jnp.int32, (1, acc.shape[0]), 1) < hole_ref[0]
    out_ref[0] = jnp.where(live, acc[...].T, 0.0).astype(BF16)

    for copies in (sends, across, beside, onward):
        for copy in copies.values():
            copy.wait_send()


def on_device(n_chan, n_kred, t2_ph, dest_owner, source_owner, source_slot, hole_count, ladder_v):
    slab, width = t2_ph.shape[1:]
    capacity = 2 * slab // n_chan
    capacity = -(-capacity // 16) * 16
    total = ladder_v.shape[1]
    wide = 256 if slab % 256 == 0 else slab
    pieces = slab // wide
    n_outer = n_kred // 2
    vmem = pl.BlockSpec(memory_space=pltpu.VMEM)
    dma = pltpu.SemaphoreType.DMA
    return pl.pallas_call(
        functools.partial(kernel, n_chan, n_kred),
        out_shape=jax.ShapeDtypeStruct((1, slab, width), BF16),
        in_specs=[
            vmem,
            vmem,
            vmem,
            vmem,
            pl.BlockSpec(memory_space=pltpu.SMEM),
            pl.BlockSpec(memory_space=pl.ANY),
        ],
        out_specs=vmem,
        scratch_shapes=[
            pltpu.VMEM((n_chan, capacity, width), BF16),
            pltpu.VMEM((n_chan, capacity, width), BF16),
            pltpu.VMEM((n_chan, capacity, slab), BF16),
            pltpu.VMEM((n_kred, pieces, width, wide), BF16),
            pltpu.VMEM((total, slab), BF16),
            pltpu.VMEM((width, slab), F32),
            pltpu.VMEM((width, slab), F32),
            dma,
            dma((n_chan,)),
            dma((n_chan,)),
            dma((n_outer, pieces)),
            dma((n_outer, pieces)),
            dma((pieces,)),
            dma((pieces,)),
            dma((n_outer, pieces)),
            dma((n_outer, pieces)),
        ],
        compiler_params=pltpu.CompilerParams(
            collective_id=0, has_side_effects=True, vmem_limit_bytes=56 * 2**20
        ),
        cost_estimate=pl.CostEstimate(
            flops=2 * total * slab * width, bytes_accessed=2 * total * slab, transcendentals=0
        ),
    )(t2_ph, dest_owner, source_owner, source_slot, hole_count, ladder_v)


def solution(mesh):
    placed = (
        P("chan", "kred", None),
        P("chan", "kred"),
        P("chan", "kred"),
        P("chan", "kred"),
        P("chan"),
        P("chan", None, "kred"),
    )
    return jax.shard_map(
        functools.partial(on_device, mesh.shape["chan"], mesh.shape["kred"]),
        mesh=mesh,
        in_specs=placed,
        out_specs=P("chan", "kred", None),
        check_vma=False,
    )
```

time: 70.5 us -> 30.9 us (0.44)
  waiting for transfers between devices: 29 us -> 0 us
  Pallas kernels: 0 us -> 28.4 us
  between operations: 14.1 us -> 0.66 us
  local copies, waits for them, and re-layouts: 9.41 us -> 1.67 us
  starting transfers between devices: 7.29 us -> 0 us
  other arithmetic: 5.36 us -> 0 us
  matrix products: 4.99 us -> 0 us
    pallas_call x0 -> x1, Pallas kernels: none -> 28.4 us  [on_device(): pl.pallas_call(functools.partial(kernel, n_chan, n_kred), out_shape=jax.S...]
    all_gather x1 -> x0, waiting for transfers between devices: 15.3 us -> none  [on_device(): lax.all_gather(recoupled, 'kred', axis=0, tiled=True)]
    all_to_all x1 -> x0, waiting for transfers between devices: 13.7 us -> none  [on_device(): lax.all_to_all(outbox.reshape(owners_count, capacity, hole_width), 'chan'...]
    all_to_all x1 -> x0, starting transfers between devices: 7.25 us -> none  [on_device(): lax.all_to_all(outbox.reshape(owners_count, capacity, hole_width), 'chan'...]
    dot_general x1 -> x0, matrix products: 4.99 us -> none  [on_device(): lax.dot_general(weights, lax.all_gather(recoupled, 'kred', axis=0, tiled=...]
    gather x1 -> x0, local copies, waits for them, and re-layouts: 4.31 us -> none  [on_device(): recoupled = arrived.reshape(owners_count * capacity, hole_width)[picked]]
    scatter x1 -> x0, local copies, waits for them, and re-layouts: 3.98 us -> none  [on_device(): jnp.zeros((owners_count * capacity, hole_width), ph_rows.dtype).at[target]]
    another operation x2 -> x0, other arithmetic: 2.41 us -> none
  transfers between devices with their start and end apart: 2 -> 0, of which waited for: 2 -> 0; matrix products, arithmetic and copies ran while one was open for 1% -> 0% of each run, Pallas kernels for 0% -> 0%
where the time goes in v1:
time: 30.9 us; the launch traced here: 30.7 us
  Pallas kernels  28.4 us (92%)
  local copies, waits for them, and re-layouts  1.67 us (5%)
  between operations  0.66 us (2%)
    pallas_call x1, Pallas kernels, on_device(): pl.pallas_call(functools.partial(kernel, n_chan, n_kred), out_shape=jax.S...  28.4 us
    unnamed x1, local copies, waits for them, and re-layouts  1.67 us

profile of v1, /device:TPU:0, one launch (start us, length us, event | category | flops | bytes accessed | tf_op | source)
XLA Modules:
  0.0 30.7 jit_solution(8189310216305580526)
XLA Ops:
  0.7 28.4 %shard_map.64 = bf16[1,1024,128]{2,1,0:T(8,128)(2,1)} custom-call(bf16[1,1024,128]{2,1,0:T(8,128)(2,1)} %t2_ref.1, s32[1,1024]{1,0:T(1,128)} %dest_ref.1, s32[1,1024]{1,0:T(1,128)} %owner_ref.1, s32[1,1024]{1,0:T(1,128)} %slot_ref.1, s32[1]{0:T(128)S(6)} %copy.8.hole_ref, bf16[1,4096,1024]{2,1,0:T(8,128)(2,1)} %v_hbm.1), custom_call_target="tpu_custom_call" | custom-call | flops 1073741824 | bytes 8388608 | tf_op jit(solution)/shard_map/pallas_call | solution.py:221
  29.0 1.7 %copy.9 = bf16[1,1024,128]{2,1,0:T(8,128)(2,1)} copy(bf16[1,1024,128]{2,1,0:T(8,128)(2,1)} %shard_map.64) | data formatting | bytes 524288

commit v2 on v1

v2 whole, which is shorter than its diff:
```python
import functools

import jax
import jax.numpy as jnp
from jax import lax
from jax.experimental import pallas as pl
from jax.experimental.pallas import tpu as pltpu
from jax.sharding import PartitionSpec as P

MESH = pl.DeviceIdType.MESH
F32 = jnp.float32
BF16 = jnp.bfloat16


def one_hot(count, row):
    lanes = row.shape[1]
    index = lax.broadcasted_iota(jnp.int32, (count, lanes), 0)
    if count <= 256:
        hit = index.astype(F32).astype(BF16) == row.astype(F32).astype(BF16)
    else:
        hit = index == row
    return jnp.where(hit, jnp.ones((), BF16), jnp.zeros((), BF16))


def row_numbers(owners, n_chan):
    rows = owners.shape[1]
    blocks = rows // 128
    channel = lax.broadcasted_iota(jnp.int32, (n_chan, 128), 0)
    hits = [
        (owners[:, b * 128 : (b + 1) * 128] == channel).astype(F32) for b in range(blocks)
    ]
    above = lax.broadcasted_iota(jnp.int32, (128, 128), 0) < lax.broadcasted_iota(
        jnp.int32, (128, 128), 1
    )
    inside = jnp.dot(
        jnp.concatenate(hits, axis=0).astype(BF16),
        jnp.where(above, 1.0, 0.0).astype(BF16),
        preferred_element_type=F32,
    )
    numbers = []
    offset = jnp.zeros((n_chan, 1), F32)
    for b in range(blocks):
        here = inside[b * n_chan : (b + 1) * n_chan] + offset
        numbers.append(jnp.sum(here * hits[b], axis=0, keepdims=True))
        offset = offset + jnp.sum(hits[b], axis=1, keepdims=True)
    return jnp.concatenate(numbers, axis=1).astype(jnp.int32)


def partners(me, n_chan):
    if n_chan & (n_chan - 1) == 0:

        def flipped(step):
            index, bit = 0, 1
            while bit < n_chan:
                index = index + ((me // bit + step // bit) % 2) * bit
                bit *= 2
            return index

        far = list(range(n_chan // 2, n_chan))
        near = list(range(1, n_chan // 2))
        order = []
        while far or near:
            order += far[:2] if not order else far[:1]
            far = far[2:] if len(order) == 2 else far[1:]
            order += near[:1]
            near = near[1:]
        return flipped, flipped, order
    return (
        lambda step: (me + step) % n_chan,
        lambda step: (me - step + n_chan) % n_chan,
        list(range(1, n_chan)),
    )


def kernel(
    n_chan,
    n_kred,
    t2_hbm,
    dest_hbm,
    owner_hbm,
    slot_hbm,
    hole_hbm,
    v_hbm,
    out_ref,
    t2_ref,
    dest_ref,
    lists,
    hole_ref,
    outbox,
    arrived,
    passed,
    picks,
    slabs,
    v_ref,
    acc,
    part,
    in_sem,
    v_sem,
    a_send,
    a_recv,
    p_send,
    p_recv,
    l_send,
    l_recv,
    s_send,
    s_recv,
):
    chan = lax.axis_index("chan")
    kred = lax.axis_index("kred")
    n_outer = n_kred // 2
    inner = kred % 2
    outer = kred // 2
    sibling = {"kred": outer * 2 + (1 - inner)}
    capacity = outbox.shape[1]
    slab = t2_ref.shape[0]
    pieces, wide = slabs.shape[1], slabs.shape[3]
    receiver, sender, order = partners(chan, n_chan)

    def beyond(d):
        return {"kred": ((outer + d) % n_outer) * 2 + inner}

    load_dest = pltpu.make_async_copy(dest_hbm, dest_ref, in_sem.at[0])
    load_t2 = pltpu.make_async_copy(t2_hbm.at[0], t2_ref, in_sem.at[1])
    load_owner = pltpu.make_async_copy(owner_hbm, lists.at[0, 0], in_sem.at[2])
    load_slot = pltpu.make_async_copy(slot_hbm, lists.at[0, 1], in_sem.at[3])
    load_hole = pltpu.make_async_copy(hole_hbm, hole_ref, in_sem.at[4])
    load_v = pltpu.make_async_copy(v_hbm.at[0], v_ref, v_sem)
    load_dest.start()
    load_t2.start()
    load_owner.start()
    load_slot.start()
    load_hole.start()

    barrier = pltpu.get_barrier_semaphore()
    for o in order:
        pl.semaphore_signal(
            barrier, inc=1, device_id={"chan": receiver(o)}, device_id_type=MESH
        )
    pl.semaphore_signal(barrier, inc=1, device_id=sibling, device_id_type=MESH)
    for d in range(1, n_outer):
        pl.semaphore_signal(barrier, inc=1, device_id=beyond(d), device_id_type=MESH)

    load_dest.wait()
    owners = dest_ref[...]
    numbers = row_numbers(owners, n_chan)
    load_t2.wait()
    rows = t2_ref[...]

    def packed(channel):
        choose = one_hot(capacity, jnp.where(owners == channel, numbers, -1))
        return jnp.dot(choose, rows, preferred_element_type=F32).astype(BF16)

    sends, passes, listed = {}, {}, {}
    for at, o in enumerate(order):
        outbox[o] = packed(receiver(o))
        if at == 0:
            pl.semaphore_wait(barrier, n_chan - 1 + 1 + n_outer - 1)
        sends[o] = pltpu.make_async_remote_copy(
            src_ref=outbox.at[o],
            dst_ref=arrived.at[o],
            send_sem=a_send.at[o],
            recv_sem=a_recv.at[o],
            device_id={"chan": receiver(o)},
            device_id_type=MESH,
        )
        sends[o].start()
    load_v.start()
    arrived[0] = packed(chan)

    def pass_on(o):
        for d in range(1, n_outer):
            passes[d, o] = pltpu.make_async_remote_copy(
                src_ref=arrived.at[o],
                dst_ref=passed.at[d, o],
                send_sem=p_send.at[d, o],
                recv_sem=p_recv.at[d, o],
                device_id=beyond(d),
                device_id_type=MESH,
            )
            passes[d, o].start()

    load_owner.wait()
    load_slot.wait()
    for d in range(1, n_outer):
        listed[d] = pltpu.make_async_remote_copy(
            src_ref=lists.at[0],
            dst_ref=lists.at[d],
            send_sem=l_send.at[d],
            recv_sem=l_recv.at[d],
            device_id=beyond(d),
            device_id_type=MESH,
        )
        listed[d].start()
    pass_on(0)

    def lay_out(d):
        for o in [0] + order:
            mine = jnp.where(lists[d, 0] == sender(o), lists[d, 1], -1)
            picks[d, o] = one_hot(capacity, mine)

    def spread(d, o):
        block = arrived[o] if d == 0 else passed[d, o]
        term = lax.dot_general(
            block, picks[d, o], (((0,), (0,)), ((), ())), preferred_element_type=F32
        )
        if o == 0:
            part[d] = term
        else:
            part[d] += term

    shares = {}

    def finish(d):
        for i in range(pieces):
            slabs[2 * d, i] = part[d, :, i * wide : (i + 1) * wide].astype(BF16)
            shares[d, i] = pltpu.make_async_remote_copy(
                src_ref=slabs.at[2 * d, i],
                dst_ref=slabs.at[2 * d + 1, i],
                send_sem=s_send.at[d, i],
                recv_sem=s_recv.at[d, i],
                device_id=sibling,
                device_id_type=MESH,
            )
            shares[d, i].start()

    def product(d, i, theirs):
        index = ((outer - d + n_outer) % n_outer) * 2
        index = index + (1 - inner if theirs else inner)
        start = pl.multiple_of(index * slab + i * wide, wide)
        return jnp.dot(
            slabs[2 * d + theirs, i], v_ref[pl.ds(start, wide), :], preferred_element_type=F32
        )

    lay_out(0)
    for d in range(1, n_outer):
        listed[d].wait_recv()
        lay_out(d)
    steps = [0] + order
    lag = 2
    for at, o in enumerate(steps):
        if o:
            sends[o].wait_recv()
            pass_on(o)
        spread(0, o)
        if lag <= at < len(steps) - 1:
            for d in range(1, n_outer):
                passes[d, steps[at - lag]].wait_recv()
                spread(d, steps[at - lag])
    finish(0)
    load_v.wait()
    for d in range(1, n_outer):
        for o in steps[max(len(steps) - 1 - lag, 0) : -1]:
            passes[d, o].wait_recv()
            spread(d, o)
    acc[...] = product(0, 0, 0)
    for i in range(1, pieces):
        acc[...] += product(0, i, 0)
    for d in range(1, n_outer):
        passes[d, steps[-1]].wait_recv()
        spread(d, steps[-1])
        finish(d)
    for i in range(pieces):
        shares[0, i].wait_recv()
        acc[...] += product(0, i, 1)
    for d in range(1, n_outer):
        for i in range(pieces):
            acc[...] += product(d, i, 0)
        for i in range(pieces):
            shares[d, i].wait_recv()
            acc[...] += product(d, i, 1)

    load_hole.wait()
    live = lax.broadcasted_iota(jnp.int32, (1, acc.shape[0]), 1) < hole_ref[0]
    out_ref[0] = jnp.where(live, acc[...].T, 0.0).astype(BF16)

    for copies in (sends, listed, passes, shares):
        for copy in copies.values():
            copy.wait_send()


def on_device(n_chan, n_kred, t2_ph, dest_owner, source_owner, source_slot, hole_count, ladder_v):
    slab, width = t2_ph.shape[1:]
    capacity = 2 * slab // n_chan
    capacity = -(-capacity // 16) * 16
    total = ladder_v.shape[1]
    wide = 256 if slab % 256 == 0 else slab
    pieces = slab // wide
    n_outer = n_kred // 2
    dma = pltpu.SemaphoreType.DMA
    return pl.pallas_call(
        functools.partial(kernel, n_chan, n_kred),
        out_shape=pltpu.VMEM((1, slab, width), BF16),
        in_specs=[pl.BlockSpec(memory_space=pltpu.HBM)] * 6,
        out_specs=pl.BlockSpec(memory_space=pltpu.VMEM),
        scratch_shapes=[
            pltpu.VMEM((slab, width), BF16),
            pltpu.VMEM((1, slab), jnp.int32),
            pltpu.VMEM((n_outer, 2, 1, slab), jnp.int32),
            pltpu.SMEM((1,), jnp.int32),
            pltpu.VMEM((n_chan, capacity, width), BF16),
            pltpu.VMEM((n_chan, capacity, width), BF16),
            pltpu.VMEM((n_outer, n_chan, capacity, width), BF16),
            pltpu.VMEM((n_outer, n_chan, capacity, slab), BF16),
            pltpu.VMEM((n_kred, pieces, width, wide), BF16),
            pltpu.VMEM((total, slab), BF16),
            pltpu.VMEM((width, slab), F32),
            pltpu.VMEM((n_outer, width, slab), F32),
            dma((5,)),
            dma,
            dma((n_chan,)),
            dma((n_chan,)),
            dma((n_outer, n_chan)),
            dma((n_outer, n_chan)),
            dma((n_outer,)),
            dma((n_outer,)),
            dma((n_outer, pieces)),
            dma((n_outer, pieces)),
        ],
        compiler_params=pltpu.CompilerParams(
            collective_id=0, has_side_effects=True, vmem_limit_bytes=56 * 2**20
        ),
        cost_estimate=pl.CostEstimate(
            flops=2 * total * slab * width, bytes_accessed=2 * total * slab, transcendentals=0
        ),
    )(t2_ph, dest_owner, source_owner, source_slot, hole_count, ladder_v)


def solution(mesh):
    placed = (
        P("chan", "kred", None),
        P("chan", "kred"),
        P("chan", "kred"),
        P("chan", "kred"),
        P("chan"),
        P("chan", None, "kred"),
    )
    return jax.shard_map(
        functools.partial(on_device, mesh.shape["chan"], mesh.shape["kred"]),
        mesh=mesh,
        in_specs=placed,
        out_specs=P("chan", "kred", None),
        check_vma=False,
    )
```

time: 30.9 us -> 30.7 us (level)
  local copies, waits for them, and re-layouts: 1.67 us -> 0.71 us
  Pallas kernels: 28.4 us -> 29.1 us
    unnamed x1, local copies, waits for them, and re-layouts: 1.67 us -> 0.71 us
    pallas_call x1, Pallas kernels: 28.4 us -> 29.1 us  [on_device(): pl.pallas_call(functools.partial(kernel, n_chan, n_kred), out_shape=pltpu...]
where the time goes in v2:
time: 30.7 us; the launch traced here: 30.5 us
  Pallas kernels  29.1 us (95%)
  local copies, waits for them, and re-layouts  0.71 us (2%)
  between operations  0.66 us (2%)
    pallas_call x1, Pallas kernels, on_device(): pl.pallas_call(functools.partial(kernel, n_chan, n_kred), out_shape=pltpu...  29.1 us
    unnamed x1, local copies, waits for them, and re-layouts  0.71 us

profile of v2, /device:TPU:0, one launch (start us, length us, event | category | flops | bytes accessed | tf_op | source)
XLA Modules:
  0.0 30.5 jit_solution(14937792355910294573)
XLA Ops:
  0.7 29.1 %shard_map.64 = bf16[1,1024,128]{2,1,0:T(8,128)(2,1)S(1)} custom-call(bf16[1,1024,128]{2,1,0:T(8,128)(2,1)} %t2_hbm.1, s32[1,1024]{1,0:T(1,128)} %dest_hbm.1, s32[1,1024]{1,0:T(1,128)} %owner_hbm.1, s32[1,1024]{1,0:T(1,128)} %slot_hbm.1, s32[1]{0:T(128)S(6)} %copy.9.hole_hbm, bf16[1,4096,1024]{2,1,0:T(8,128)(2,1)} %v_hbm.1), custom_call_target="tpu_custom_call" | custom-call | flops 1073741824 | bytes 8388608 | tf_op jit(solution)/shard_map/pallas_call | solution.py:290
  29.8 0.7 %copy.8 = bf16[1,1024,128]{2,1,0:T(8,128)(2,1)} copy(bf16[1,1024,128]{2,1,0:T(8,128)(2,1)S(1)} %shard_map.64) | data formatting | bytes 524288

commit v3 on v2

--- a/solution.py
+++ b/solution.py
@@ -58,17 +58,12 @@
 
         far = list(range(n_chan // 2, n_chan))
         near = list(range(1, n_chan // 2))
-        order = []
-        while far or near:
-            order += far[:2] if not order else far[:1]
-            far = far[2:] if len(order) == 2 else far[1:]
-            order += near[:1]
-            near = near[1:]
-        return flipped, flipped, order
+        return flipped, flipped, near, far
     return (
         lambda step: (me + step) % n_chan,
         lambda step: (me - step + n_chan) % n_chan,
         list(range(1, n_chan)),
+        [],
     )
 
 
@@ -114,7 +109,8 @@
     capacity = outbox.shape[1]
     slab = t2_ref.shape[0]
     pieces, wide = slabs.shape[1], slabs.shape[3]
-    receiver, sender, order = partners(chan, n_chan)
+    receiver, sender, near, far = partners(chan, n_chan)
+    order = near + far
 
     def beyond(d):
         return {"kred": ((outer + d) % n_outer) * 2 + inner}
@@ -151,7 +147,7 @@
         return jnp.dot(choose, rows, preferred_element_type=F32).astype(BF16)
 
     sends, passes, listed = {}, {}, {}
-    for at, o in enumerate(order):
+    for at, o in enumerate(far[:1] + near + far[1:]):
         outbox[o] = packed(receiver(o))
         if at == 0:
             pl.semaphore_wait(barrier, n_chan - 1 + 1 + n_outer - 1)
@@ -163,7 +159,8 @@
             device_id={"chan": receiver(o)},
             device_id_type=MESH,
         )
-        sends[o].start()
+        if o not in far[1:]:
+            sends[o].start()
     load_v.start()
     arrived[0] = packed(chan)
 
@@ -241,6 +238,9 @@
         if o:
             sends[o].wait_recv()
             pass_on(o)
+        if o in far[:-1]:
+            sends[o].wait_send()
+            sends[o + 1].start()
         spread(0, o)
         if lag <= at < len(steps) - 1:
             for d in range(1, n_outer):
@@ -273,7 +273,9 @@
     live = lax.broadcasted_iota(jnp.int32, (1, acc.shape[0]), 1) < hole_ref[0]
     out_ref[0] = jnp.where(live, acc[...].T, 0.0).astype(BF16)
 
-    for copies in (sends, listed, passes, shares):
+    for o in near + far[-1:]:
+        sends[o].wait_send()
+    for copies in (listed, passes, shares):
         for copy in copies.values():
             copy.wait_send()
 

time: 30.7 us -> 35.1 us (1.14)
  Pallas kernels: 29.1 us -> 33.5 us
    pallas_call x1, Pallas kernels: 29.1 us -> 33.5 us  [on_device(): pl.pallas_call(functools.partial(kernel, n_chan, n_kred), out_shape=pltpu...]
where the time goes in v3:
time: 35.1 us; the launch traced here: 34.9 us
  Pallas kernels  33.5 us (95%)
  local copies, waits for them, and re-layouts  0.71 us (2%)
  between operations  0.66 us (2%)
    pallas_call x1, Pallas kernels, on_device(): pl.pallas_call(functools.partial(kernel, n_chan, n_kred), out_shape=pltpu...  33.5 us
    unnamed x1, local copies, waits for them, and re-layouts  0.71 us

profile of v3, /device:TPU:0, one launch (start us, length us, event | category | flops | bytes accessed | tf_op | source)
XLA Modules:
  0.0 34.9 jit_solution(8351022301241265650)
XLA Ops:
  0.7 33.5 %shard_map.64 = bf16[1,1024,128]{2,1,0:T(8,128)(2,1)S(1)} custom-call(bf16[1,1024,128]{2,1,0:T(8,128)(2,1)} %t2_hbm.1, s32[1,1024]{1,0:T(1,128)} %dest_hbm.1, s32[1,1024]{1,0:T(1,128)} %owner_hbm.1, s32[1,1024]{1,0:T(1,128)} %slot_hbm.1, s32[1]{0:T(128)S(6)} %copy.9.hole_hbm, bf16[1,4096,1024]{2,1,0:T(8,128)(2,1)} %v_hbm.1), custom_call_target="tpu_custom_call" | custom-call | flops 1073741824 | bytes 8388608 | tf_op jit(solution)/shard_map/pallas_call | solution.py:292
  34.2 0.7 %copy.8 = bf16[1,1024,128]{2,1,0:T(8,128)(2,1)} copy(bf16[1,1024,128]{2,1,0:T(8,128)(2,1)S(1)} %shard_map.64) | data formatting | bytes 524288

commit v4 on v3

v4 whole, which is shorter than its diff:
```python
import functools

import jax
import jax.numpy as jnp
from jax import lax
from jax.experimental import pallas as pl
from jax.experimental.pallas import tpu as pltpu
from jax.sharding import PartitionSpec as P

MESH = pl.DeviceIdType.MESH
F32 = jnp.float32
BF16 = jnp.bfloat16


def one_hot(count, row):
    lanes = row.shape[1]
    index = lax.broadcasted_iota(jnp.int32, (count, lanes), 0)
    if count <= 256:
        hit = index.astype(F32).astype(BF16) == row.astype(F32).astype(BF16)
    else:
        hit = index == row
    return jnp.where(hit, jnp.ones((), BF16), jnp.zeros((), BF16))


def row_numbers(owners, n_chan):
    rows = owners.shape[1]
    blocks = rows // 128
    channel = lax.broadcasted_iota(jnp.int32, (n_chan, 128), 0)
    hits = [
        (owners[:, b * 128 : (b + 1) * 128] == channel).astype(F32) for b in range(blocks)
    ]
    above = lax.broadcasted_iota(jnp.int32, (128, 128), 0) < lax.broadcasted_iota(
        jnp.int32, (128, 128), 1
    )
    inside = jnp.dot(
        jnp.concatenate(hits, axis=0).astype(BF16),
        jnp.where(above, 1.0, 0.0).astype(BF16),
        preferred_element_type=F32,
    )
    numbers = []
    offset = jnp.zeros((n_chan, 1), F32)
    for b in range(blocks):
        here = inside[b * n_chan : (b + 1) * n_chan] + offset
        numbers.append(jnp.sum(here * hits[b], axis=0, keepdims=True))
        offset = offset + jnp.sum(hits[b], axis=1, keepdims=True)
    return jnp.concatenate(numbers, axis=1).astype(jnp.int32)


def partners(me, n_chan):
    if n_chan & (n_chan - 1) == 0:

        def flipped(step):
            index, bit = 0, 1
            while bit < n_chan:
                index = index + ((me // bit + step // bit) % 2) * bit
                bit *= 2
            return index

        far = list(range(n_chan // 2, n_chan))
        near = list(range(1, n_chan // 2))
        return flipped, flipped, near, far
    return (
        lambda step: (me + step) % n_chan,
        lambda step: (me - step + n_chan) % n_chan,
        list(range(1, n_chan)),
        [],
    )


def kernel(
    n_chan,
    n_kred,
    t2_hbm,
    dest_hbm,
    owner_hbm,
    slot_hbm,
    hole_hbm,
    v_hbm,
    out_ref,
    t2_ref,
    dest_ref,
    lists,
    hole_ref,
    outbox,
    arrived,
    picks,
    slabs,
    v_ref,
    acc,
    part,
    in_sem,
    v_sem,
    a_send,
    a_recv,
    y_send,
    y_recv,
    s_send,
    s_recv,
    f_send,
    f_recv,
):
    chan = lax.axis_index("chan")
    kred = lax.axis_index("kred")
    n_outer = n_kred // 2
    inner = kred % 2
    outer = kred // 2
    sibling = {"kred": outer * 2 + (1 - inner)}
    parts, tall, capacity = outbox.shape[1:]
    slab = t2_ref.shape[0]
    pieces, wide = slabs.shape[2], slabs.shape[4]
    receiver, sender, near, far = partners(chan, n_chan)
    order = near + far

    def beyond(d):
        return {"kred": ((outer + d) % n_outer) * 2 + inner}

    load_dest = pltpu.make_async_copy(dest_hbm, dest_ref, in_sem.at[0])
    load_t2 = pltpu.make_async_copy(t2_hbm.at[0], t2_ref, in_sem.at[1])
    load_owner = pltpu.make_async_copy(owner_hbm, lists.at[0], in_sem.at[2])
    load_slot = pltpu.make_async_copy(slot_hbm, lists.at[1], in_sem.at[3])
    load_hole = pltpu.make_async_copy(hole_hbm, hole_ref, in_sem.at[4])
    load_v = pltpu.make_async_copy(v_hbm.at[0], v_ref, v_sem)
    load_dest.start()
    load_t2.start()
    load_owner.start()
    load_slot.start()
    load_hole.start()

    barrier = pltpu.get_barrier_semaphore()
    for o in order:
        pl.semaphore_signal(
            barrier, inc=1, device_id={"chan": receiver(o)}, device_id_type=MESH
        )
    pl.semaphore_signal(barrier, inc=1, device_id=sibling, device_id_type=MESH)
    for d in range(1, n_outer):
        pl.semaphore_signal(barrier, inc=1, device_id=beyond(d), device_id_type=MESH)

    load_dest.wait()
    owners = dest_ref[...]
    numbers = row_numbers(owners, n_chan)
    load_t2.wait()
    rows = t2_ref[...]

    def pack(target, o, channel):
        choose = one_hot(capacity, jnp.where(owners == channel, numbers, -1))
        block = jnp.dot(choose, rows, preferred_element_type=F32).T.astype(BF16)
        for j in range(parts):
            target[o, j] = block[j * tall : (j + 1) * tall]

    sends = {}
    for at, o in enumerate(far + near):
        pack(outbox, o, receiver(o))
        if at == 0:
            pl.semaphore_wait(barrier, n_chan - 1 + 1 + n_outer - 1)
        for j in range(parts):
            sends[j, o] = pltpu.make_async_remote_copy(
                src_ref=outbox.at[o, j],
                dst_ref=arrived.at[o, j],
                send_sem=a_send.at[j, o],
                recv_sem=a_recv.at[j, o],
                device_id={"chan": receiver(o)},
                device_id_type=MESH,
            )
        sends[0, o].start()
    load_v.start()
    pack(arrived, 0, chan)
    load_owner.wait()
    load_slot.wait()
    for o in [0] + order:
        picks[o] = one_hot(capacity, jnp.where(lists[0] == sender(o), lists[1], -1))

    def spread(j, o, cols):
        return jnp.dot(arrived[o, j], picks[o, :, cols], preferred_element_type=F32)

    across, beside, onward = {}, {}, {}

    def gather(j):
        everything = slice(0, slab)
        part[...] = spread(j, 0, everything)
        for o in order[:-1]:
            sends[j, o].wait_recv()
            part[...] += spread(j, o, everything)
        if order:
            sends[j, order[-1]].wait_recv()
        for i in range(pieces):
            cols = slice(i * wide, (i + 1) * wide)
            slabs[0, j, i] = (part[:, cols] + spread(j, order[-1], cols)).astype(BF16)
            for d in range(1, n_outer):
                across[d, j, i] = pltpu.make_async_remote_copy(
                    src_ref=slabs.at[0, j, i],
                    dst_ref=slabs.at[2 * d, j, i],
                    send_sem=y_send.at[d, j, i],
                    recv_sem=y_recv.at[d, j, i],
                    device_id=beyond(d),
                    device_id_type=MESH,
                )
                across[d, j, i].start()
            beside[j, i] = pltpu.make_async_remote_copy(
                src_ref=slabs.at[0, j, i],
                dst_ref=slabs.at[1, j, i],
                send_sem=s_send.at[j, i],
                recv_sem=s_recv.at[j, i],
                device_id=sibling,
                device_id_type=MESH,
            )
            beside[j, i].start()

    def forward(d, j, i):
        across[d, j, i].wait_recv()
        onward[d, j, i] = pltpu.make_async_remote_copy(
            src_ref=slabs.at[2 * d, j, i],
            dst_ref=slabs.at[2 * d + 1, j, i],
            send_sem=f_send.at[d, j, i],
            recv_sem=f_recv.at[d, j, i],
            device_id=sibling,
            device_id_type=MESH,
        )
        onward[d, j, i].start()

    def product(d, i, theirs):
        index = ((outer - d + n_outer) % n_outer) * 2
        index = index + (1 - inner if theirs else inner)
        start = pl.multiple_of(index * slab + i * wide, wide)
        left = jnp.concatenate([slabs[2 * d + theirs, j, i] for j in range(parts)], axis=0)
        return jnp.dot(left, v_ref[pl.ds(start, wide), :], preferred_element_type=F32)

    for j in range(parts):
        if j + 1 < parts:
            for o in order:
                sends[j, o].wait_send()
                sends[j + 1, o].start()
        gather(j)
    load_v.wait()
    for j in range(parts - 1):
        for d in range(1, n_outer):
            for i in range(pieces):
                forward(d, j, i)
    acc[...] = product(0, 0, 0)
    for i in range(1, pieces):
        acc[...] += product(0, i, 0)
    for i in range(pieces):
        for j in range(parts):
            beside[j, i].wait_recv()
        acc[...] += product(0, i, 1)
    for d in range(1, n_outer):
        for i in range(pieces + 1):
            if i < pieces:
                forward(d, parts - 1, i)
                acc[...] += product(d, i, 0)
            if i:
                for j in range(parts):
                    onward[d, j, i - 1].wait_recv()
                acc[...] += product(d, i - 1, 1)

    load_hole.wait()
    live = lax.broadcasted_iota(jnp.int32, (1, acc.shape[0]), 1) < hole_ref[0]
    out_ref[0] = jnp.where(live, acc[...].T, 0.0).astype(BF16)

    for o in order:
        sends[parts - 1, o].wait_send()
    for copies in (across, beside, onward):
        for copy in copies.values():
            copy.wait_send()


def on_device(n_chan, n_kred, t2_ph, dest_owner, source_owner, source_slot, hole_count, ladder_v):
    slab, width = t2_ph.shape[1:]
    capacity = 2 * slab // n_chan
    capacity = -(-capacity // 16) * 16
    total = ladder_v.shape[1]
    wide = 256 if slab % 256 == 0 else slab
    pieces = slab // wide
    n_outer = n_kred // 2
    parts = 2
    tall = width // parts
    dma = pltpu.SemaphoreType.DMA
    return pl.pallas_call(
        functools.partial(kernel, n_chan, n_kred),
        out_shape=pltpu.VMEM((1, slab, width), BF16),
        in_specs=[pl.BlockSpec(memory_space=pltpu.HBM)] * 6,
        out_specs=pl.BlockSpec(memory_space=pltpu.VMEM),
        scratch_shapes=[
            pltpu.VMEM((slab, width), BF16),
            pltpu.VMEM((1, slab), jnp.int32),
            pltpu.VMEM((2, 1, slab), jnp.int32),
            pltpu.SMEM((1,), jnp.int32),
            pltpu.VMEM((n_chan, parts, tall, capacity), BF16),
            pltpu.VMEM((n_chan, parts, tall, capacity), BF16),
            pltpu.VMEM((n_chan, capacity, slab), BF16),
            pltpu.VMEM((n_kred, parts, pieces, tall, wide), BF16),
            pltpu.VMEM((total, slab), BF16),
            pltpu.VMEM((width, slab), F32),
            pltpu.VMEM((tall, slab), F32),
            dma((5,)),
            dma,
            dma((parts, n_chan)),
            dma((parts, n_chan)),
            dma((n_outer, parts, pieces)),
            dma((n_outer, parts, pieces)),
            dma((parts, pieces)),
            dma((parts, pieces)),
            dma((n_outer, parts, pieces)),
            dma((n_outer, parts, pieces)),
        ],
        compiler_params=pltpu.CompilerParams(
            collective_id=0, has_side_effects=True, vmem_limit_bytes=56 * 2**20
        ),
        cost_estimate=pl.CostEstimate(
            flops=2 * total * slab * width, bytes_accessed=2 * total * slab, transcendentals=0
        ),
    )(t2_ph, dest_owner, source_owner, source_slot, hole_count, ladder_v)


def solution(mesh):
    placed = (
        P("chan", "kred", None),
        P("chan", "kred"),
        P("chan", "kred"),
        P("chan", "kred"),
        P("chan"),
        P("chan", None, "kred"),
    )
    return jax.shard_map(
        functools.partial(on_device, mesh.shape["chan"], mesh.shape["kred"]),
        mesh=mesh,
        in_specs=placed,
        out_specs=P("chan", "kred", None),
        check_vma=False,
    )
```

time: 35.1 us -> 27.7 us (0.79)
  Pallas kernels: 33.5 us -> 26.2 us
    pallas_call x1, Pallas kernels: 33.5 us -> 26.2 us  [on_device(): pl.pallas_call(functools.partial(kernel, n_chan, n_kred), out_shape=pltpu...]
where the time goes in v4:
time: 27.7 us; the launch traced here: 27.5 us
  Pallas kernels  26.2 us (95%)
  local copies, waits for them, and re-layouts  0.71 us (3%)
  between operations  0.66 us (2%)
    pallas_call x1, Pallas kernels, on_device(): pl.pallas_call(functools.partial(kernel, n_chan, n_kred), out_shape=pltpu...  26.2 us
    unnamed x1, local copies, waits for them, and re-layouts  0.71 us

profile of v4, /device:TPU:0, one launch (start us, length us, event | category | flops | bytes accessed | tf_op | source)
XLA Modules:
  0.0 27.5 jit_solution(5461806147120009159)
XLA Ops:
  0.7 26.2 %shard_map.64 = bf16[1,1024,128]{2,1,0:T(8,128)(2,1)S(1)} custom-call(bf16[1,1024,128]{2,1,0:T(8,128)(2,1)} %t2_hbm.1, s32[1,1024]{1,0:T(1,128)} %dest_hbm.1, s32[1,1024]{1,0:T(1,128)} %owner_hbm.1, s32[1,1024]{1,0:T(1,128)} %slot_hbm.1, s32[1]{0:T(128)S(6)} %copy.9.hole_hbm, bf16[1,4096,1024]{2,1,0:T(8,128)(2,1)} %v_hbm.1), custom_call_target="tpu_custom_call" | custom-call | flops 1073741824 | bytes 8388608 | tf_op jit(solution)/shard_map/pallas_call | solution.py:277
  26.8 0.7 %copy.8 = bf16[1,1024,128]{2,1,0:T(8,128)(2,1)} copy(bf16[1,1024,128]{2,1,0:T(8,128)(2,1)S(1)} %shard_map.64) | data formatting | bytes 524288

commit v5 on v4

--- a/solution.py
+++ b/solution.py
@@ -70,17 +70,17 @@
 def kernel(
     n_chan,
     n_kred,
+    cuts,
     t2_hbm,
     dest_hbm,
     owner_hbm,
     slot_hbm,
-    hole_hbm,
+    hole_vmem,
     v_hbm,
     out_ref,
     t2_ref,
     dest_ref,
     lists,
-    hole_ref,
     outbox,
     arrived,
     picks,
@@ -105,9 +105,11 @@
     inner = kred % 2
     outer = kred // 2
     sibling = {"kred": outer * 2 + (1 - inner)}
-    parts, tall, capacity = outbox.shape[1:]
+    width, capacity = outbox.shape[1:]
+    parts = len(cuts) - 1
+    bands = [pl.ds(cuts[j], cuts[j + 1] - cuts[j]) for j in range(parts)]
     slab = t2_ref.shape[0]
-    pieces, wide = slabs.shape[2], slabs.shape[4]
+    pieces, wide = slabs.shape[1], slabs.shape[3]
     receiver, sender, near, far = partners(chan, n_chan)
     order = near + far
 
@@ -118,13 +120,11 @@
     load_t2 = pltpu.make_async_copy(t2_hbm.at[0], t2_ref, in_sem.at[1])
     load_owner = pltpu.make_async_copy(owner_hbm, lists.at[0], in_sem.at[2])
     load_slot = pltpu.make_async_copy(slot_hbm, lists.at[1], in_sem.at[3])
-    load_hole = pltpu.make_async_copy(hole_hbm, hole_ref, in_sem.at[4])
     load_v = pltpu.make_async_copy(v_hbm.at[0], v_ref, v_sem)
     load_dest.start()
     load_t2.start()
     load_owner.start()
     load_slot.start()
-    load_hole.start()
 
     barrier = pltpu.get_barrier_semaphore()
     for o in order:
@@ -143,9 +143,7 @@
 
     def pack(target, o, channel):
         choose = one_hot(capacity, jnp.where(owners == channel, numbers, -1))
-        block = jnp.dot(choose, rows, preferred_element_type=F32).T.astype(BF16)
-        for j in range(parts):
-            target[o, j] = block[j * tall : (j + 1) * tall]
+        target[o] = jnp.dot(choose, rows, preferred_element_type=F32).T.astype(BF16)
 
     sends = {}
     for at, o in enumerate(far + near):
@@ -154,8 +152,8 @@
             pl.semaphore_wait(barrier, n_chan - 1 + 1 + n_outer - 1)
         for j in range(parts):
             sends[j, o] = pltpu.make_async_remote_copy(
-                src_ref=outbox.at[o, j],
-                dst_ref=arrived.at[o, j],
+                src_ref=outbox.at[o, bands[j]],
+                dst_ref=arrived.at[o, bands[j]],
                 send_sem=a_send.at[j, o],
                 recv_sem=a_recv.at[j, o],
                 device_id={"chan": receiver(o)},
@@ -170,25 +168,26 @@
         picks[o] = one_hot(capacity, jnp.where(lists[0] == sender(o), lists[1], -1))
 
     def spread(j, o, cols):
-        return jnp.dot(arrived[o, j], picks[o, :, cols], preferred_element_type=F32)
+        return jnp.dot(arrived[o, bands[j]], picks[o, :, cols], preferred_element_type=F32)
 
     across, beside, onward = {}, {}, {}
 
     def gather(j):
         everything = slice(0, slab)
-        part[...] = spread(j, 0, everything)
+        some = pl.ds(0, cuts[j + 1] - cuts[j])
+        part[some] = spread(j, 0, everything)
         for o in order[:-1]:
             sends[j, o].wait_recv()
-            part[...] += spread(j, o, everything)
+            part[some] += spread(j, o, everything)
         if order:
             sends[j, order[-1]].wait_recv()
         for i in range(pieces):
             cols = slice(i * wide, (i + 1) * wide)
-            slabs[0, j, i] = (part[:, cols] + spread(j, order[-1], cols)).astype(BF16)
+            slabs[0, i, bands[j]] = (part[some, cols] + spread(j, order[-1], cols)).astype(BF16)
             for d in range(1, n_outer):
                 across[d, j, i] = pltpu.make_async_remote_copy(
-                    src_ref=slabs.at[0, j, i],
-                    dst_ref=slabs.at[2 * d, j, i],
+                    src_ref=slabs.at[0, i, bands[j]],
+                    dst_ref=slabs.at[2 * d, i, bands[j]],
                     send_sem=y_send.at[d, j, i],
                     recv_sem=y_recv.at[d, j, i],
                     device_id=beyond(d),
@@ -196,8 +195,8 @@
                 )
                 across[d, j, i].start()
             beside[j, i] = pltpu.make_async_remote_copy(
-                src_ref=slabs.at[0, j, i],
-                dst_ref=slabs.at[1, j, i],
+                src_ref=slabs.at[0, i, bands[j]],
+                dst_ref=slabs.at[1, i, bands[j]],
                 send_sem=s_send.at[j, i],
                 recv_sem=s_recv.at[j, i],
                 device_id=sibling,
@@ -208,8 +207,8 @@
     def forward(d, j, i):
         across[d, j, i].wait_recv()
         onward[d, j, i] = pltpu.make_async_remote_copy(
-            src_ref=slabs.at[2 * d, j, i],
-            dst_ref=slabs.at[2 * d + 1, j, i],
+            src_ref=slabs.at[2 * d, i, bands[j]],
+            dst_ref=slabs.at[2 * d + 1, i, bands[j]],
             send_sem=f_send.at[d, j, i],
             recv_sem=f_recv.at[d, j, i],
             device_id=sibling,
@@ -221,7 +220,7 @@
         index = ((outer - d + n_outer) % n_outer) * 2
         index = index + (1 - inner if theirs else inner)
         start = pl.multiple_of(index * slab + i * wide, wide)
-        left = jnp.concatenate([slabs[2 * d + theirs, j, i] for j in range(parts)], axis=0)
+        left = slabs[2 * d + theirs, i]
         return jnp.dot(left, v_ref[pl.ds(start, wide), :], preferred_element_type=F32)
 
     for j in range(parts):
@@ -252,8 +251,7 @@
                     onward[d, j, i - 1].wait_recv()
                 acc[...] += product(d, i - 1, 1)
 
-    load_hole.wait()
-    live = lax.broadcasted_iota(jnp.int32, (1, acc.shape[0]), 1) < hole_ref[0]
+    live = lax.broadcasted_iota(jnp.int32, (1, acc.shape[0]), 1) < hole_vmem[...]
     out_ref[0] = jnp.where(live, acc[...].T, 0.0).astype(BF16)
 
     for o in order:
@@ -271,27 +269,27 @@
     wide = 256 if slab % 256 == 0 else slab
     pieces = slab // wide
     n_outer = n_kred // 2
-    parts = 2
-    tall = width // parts
+    cuts = (0, -(-width * 5 // 128) * 16, width)
+    parts = len(cuts) - 1
     dma = pltpu.SemaphoreType.DMA
     return pl.pallas_call(
-        functools.partial(kernel, n_chan, n_kred),
+        functools.partial(kernel, n_chan, n_kred, cuts),
         out_shape=pltpu.VMEM((1, slab, width), BF16),
-        in_specs=[pl.BlockSpec(memory_space=pltpu.HBM)] * 6,
+        in_specs=[pl.BlockSpec(memory_space=pltpu.HBM)] * 4
+        + [pl.BlockSpec(memory_space=pltpu.VMEM), pl.BlockSpec(memory_space=pltpu.HBM)],
         out_specs=pl.BlockSpec(memory_space=pltpu.VMEM),
         scratch_shapes=[
             pltpu.VMEM((slab, width), BF16),
             pltpu.VMEM((1, slab), jnp.int32),
             pltpu.VMEM((2, 1, slab), jnp.int32),
-            pltpu.SMEM((1,), jnp.int32),
-            pltpu.VMEM((n_chan, parts, tall, capacity), BF16),
-            pltpu.VMEM((n_chan, parts, tall, capacity), BF16),
+            pltpu.VMEM((n_chan, width, capacity), BF16),
+            pltpu.VMEM((n_chan, width, capacity), BF16),
             pltpu.VMEM((n_chan, capacity, slab), BF16),
-            pltpu.VMEM((n_kred, parts, pieces, tall, wide), BF16),
+            pltpu.VMEM((n_kred, pieces, width, wide), BF16),
             pltpu.VMEM((total, slab), BF16),
             pltpu.VMEM((width, slab), F32),
-            pltpu.VMEM((tall, slab), F32),
-            dma((5,)),
+            pltpu.VMEM((width, slab), F32),
+            dma((4,)),
             dma,
             dma((parts, n_chan)),
             dma((parts, n_chan)),
@@ -308,7 +306,7 @@
         cost_estimate=pl.CostEstimate(
             flops=2 * total * slab * width, bytes_accessed=2 * total * slab, transcendentals=0
         ),
-    )(t2_ph, dest_owner, source_owner, source_slot, hole_count, ladder_v)
+    )(t2_ph, dest_owner, source_owner, source_slot, hole_count[:, None], ladder_v)
 
 
 def solution(mesh):

time: 27.7 us -> 27.7 us (level)
  no operation moved by 1% of the time
where the time goes in v5:
time: 27.7 us; the launch traced here: 27.4 us
  Pallas kernels  26 us (94%)
  local copies, waits for them, and re-layouts  0.71 us (3%)
  between operations  0.66 us (2%)
    pallas_call x1, Pallas kernels, on_device(): pl.pallas_call(functools.partial(kernel, n_chan, n_kred, cuts), out_shape...  26 us
    unnamed x1, local copies, waits for them, and re-layouts  0.71 us

profile of v5, /device:TPU:0, one launch (start us, length us, event | category | flops | bytes accessed | tf_op | source)
XLA Modules:
  0.0 27.4 jit_solution(5106920423261217450)
XLA Ops:
  0.7 26.0 %shard_map.64 = bf16[1,1024,128]{2,1,0:T(8,128)(2,1)S(1)} custom-call(bf16[1,1024,128]{2,1,0:T(8,128)(2,1)} %t2_hbm.1, s32[1,1024]{1,0:T(1,128)} %dest_hbm.1, s32[1,1024]{1,0:T(1,128)} %owner_hbm.1, s32[1,1024]{1,0:T(1,128)} %slot_hbm.1, s32[1,1]{1,0:T(1,128)} %bitcast.1.hole_vmem, bf16[1,4096,1024]{2,1,0:T(8,128)(2,1)} %v_hbm.1), custom_call_target="tpu_custom_call" | custom-call | flops 1073741824 | bytes 8388608 | tf_op jit(solution)/shard_map/pallas_call | solution.py:275
  26.7 0.7 %copy.8 = bf16[1,1024,128]{2,1,0:T(8,128)(2,1)} copy(bf16[1,1024,128]{2,1,0:T(8,128)(2,1)S(1)} %shard_map.64) | data formatting | bytes 524288
